TPU v7x, 768 devices: a whole 4x8x12 slice. The times are simulated.
768 devices in a mesh: ctx: 64 (over x, y, core), head: 12 (over z).
Axes of the slice: x: 4, y: 8, z: 12, core: 2. Of those that a mesh axis runs over, the one named last changes fastest.
Arguments:
- hidden_in: bfloat16 [12288, 4096], P('ctx'), may hold values from -10 to 10
- query_soft: bfloat16 [12288, 3072], P('ctx', 'head'), may hold values from -6 to 6
- key_soft: bfloat16 [12288, 1536], P('ctx', 'head'), may hold values from -6 to 6
- value_soft: bfloat16 [12288, 1536], P('ctx', 'head'), may hold values from -6 to 6
- out_weight: bfloat16 [3072, 4096], P('head'), may hold values from -0.109375 to 0.109375
- query_weight: bfloat16 [4096, 3072], P(None, 'head'), may hold values from -0.09375 to 0.09375
- key_weight: bfloat16 [4096, 3072], P(None, 'head'), may hold values from -0.09375 to 0.09375
- value_weight: bfloat16 [4096, 3072], P(None, 'head'), may hold values from -0.09375 to 0.09375
Outputs:
- linear_out: bfloat16 [12288, 3072], P('ctx', 'head')
All inputs are finite; a program needn't handle non-finite values.
Results may differ from a plain program's by a relative error of at most 0.025.
Values may be sent and summed in bfloat16 or wider, within the bound.
A program may use at most 64 MiB of HBM per device.

v0:
```python
import math

import jax
import jax.numpy as jnp
from jax import lax
from jax.sharding import PartitionSpec as P

HEAD_DIM = 128
HEAD_DEV = 2


def prefix(x, axis, combine, identity):
    length, position = (lax.axis_size(axis), lax.axis_index(axis))
    everything = lax.all_gather(x.astype(jnp.bfloat16), axis)
    start = jnp.broadcast_to(jnp.asarray(identity, x.dtype), x.shape)

    def lap(k, before):
        reached = k < position
        new = combine(before, everything[k].astype(x.dtype))
        return jnp.where(reached, new, before)

    return lax.fori_loop(0, length, lap, start)


def rms_rows(values):
    return values * lax.rsqrt(jnp.mean(values * values, axis=-1, keepdims=True) + 1e-06)


def add_states(earlier, later):
    return earlier + later


def attend_block(carry, key_rows, value_rows, key_start, query_pos, queries, masked):
    run_max, run_sum, run_out = carry
    scores = jnp.einsum("qhd,kd->hqk", queries, key_rows, preferred_element_type=jnp.float32) * (
        1.0 / math.sqrt(HEAD_DIM)
    )
    if masked:
        key_pos = key_start + lax.iota(jnp.int32, key_rows.shape[0])
        allowed = key_pos[None, None, :] <= query_pos[None, :, None]
        fresh_max = jnp.maximum(run_max, jnp.max(jnp.where(allowed, scores, -1e30), axis=-1))
        weights = jnp.where(allowed, jnp.exp(scores - fresh_max[:, :, None]), 0.0)
    else:
        fresh_max = jnp.maximum(run_max, jnp.max(scores, axis=-1))
        weights = jnp.exp(scores - fresh_max[:, :, None])
    factor = jnp.exp(run_max - fresh_max)
    run_sum = run_sum * factor + jnp.sum(weights, axis=-1)
    run_out = run_out * factor[:, :, None] + jnp.einsum(
        "hqk,kd->hqd", weights.astype(jnp.bfloat16), value_rows, preferred_element_type=jnp.float32
    )
    return (fresh_max, run_sum, run_out)


def largest_divisor(whole, limit):
    best = 1
    for trial in range(1, min(whole, limit) + 1):
        if whole % trial == 0:
            best = trial
    return best


def fold_keys(carry, pieces, queries, query_pos, row_count):
    key_part, value_part = pieces
    shards = key_part.shape[0] // row_count
    per_step = largest_divisor(shards, max(1, 2048 // row_count))
    key_span = per_step * row_count
    block_count = shards // per_step
    key_blocks = key_part.reshape(block_count, key_span, key_part.shape[1])
    value_blocks = value_part.reshape(block_count, key_span, value_part.shape[1])
    first_query = query_pos[0]
    last_query = query_pos[-1]

    def step_fn(carry_now, block_item):
        key_rows, value_rows, block_index = block_item
        key_start = block_index * key_span
        key_end = key_start + key_span - 1
        branch_index = jnp.where(
            key_end <= first_query, 0, jnp.where(key_start <= last_query, 1, 2)
        ).astype(jnp.int32)
        result = lax.switch(
            branch_index,
            [
                lambda inner: attend_block(
                    inner, key_rows, value_rows, key_start, query_pos, queries, False
                ),
                lambda inner: attend_block(
                    inner, key_rows, value_rows, key_start, query_pos, queries, True
                ),
                lambda inner: inner,
            ],
            carry_now,
        )
        return (result, None)

    carry, unused = lax.scan(
        step_fn, carry, (key_blocks, value_blocks, jnp.arange(block_count, dtype=jnp.int32))
    )
    return carry


def body(
    hidden_in, query_soft, key_soft, value_soft, out_weight, query_weight, key_weight, value_weight
):
    row_count = hidden_in.shape[0]
    head_width = HEAD_DEV * HEAD_DIM
    queries = query_soft.reshape(row_count, HEAD_DEV, HEAD_DIM)
    query_pos = lax.axis_index("ctx") * row_count + lax.iota(jnp.int32, row_count)
    start_carry = (
        jnp.full((HEAD_DEV, row_count), -1e30, jnp.float32),
        jnp.zeros((HEAD_DEV, row_count), jnp.float32),
        jnp.zeros((HEAD_DEV, row_count, HEAD_DIM), jnp.float32),
    )
    run_max, run_sum, run_out = fold_keys(
        start_carry,
        (
            lax.all_gather(key_soft, "ctx", axis=0, tiled=True),
            lax.all_gather(value_soft, "ctx", axis=0, tiled=True),
        ),
        queries,
        query_pos,
        row_count,
    )
    attended = (run_out / run_sum[:, :, None]).astype(jnp.bfloat16)
    attended = jnp.transpose(attended, (1, 0, 2)).reshape(row_count, head_width)
    summed = lax.psum(
        jnp.dot(attended, out_weight, preferred_element_type=jnp.float32).astype(jnp.bfloat16),
        "head",
    ).astype(jnp.float32)
    normed = rms_rows(hidden_in.astype(jnp.float32) + summed).astype(jnp.bfloat16)
    projected = jnp.concatenate(
        [
            jnp.dot(normed, query_weight, preferred_element_type=jnp.float32),
            jnp.dot(normed, key_weight, preferred_element_type=jnp.float32),
            jnp.dot(normed, value_weight, preferred_element_type=jnp.float32),
        ],
        axis=1,
    ).astype(jnp.bfloat16)
    lin_query = projected[:, :head_width].reshape(row_count, HEAD_DEV, HEAD_DIM)
    lin_key = projected[:, head_width : 2 * head_width].reshape(row_count, HEAD_DEV, HEAD_DIM)
    lin_value = projected[:, 2 * head_width :].reshape(row_count, HEAD_DEV, HEAD_DIM)
    block_state = jnp.einsum("thd,the->hde", lin_key, lin_value, preferred_element_type=jnp.float32)
    carried = prefix(block_state, "ctx", add_states, jnp.zeros_like(block_state)).astype(
        jnp.bfloat16
    )
    carried_part = jnp.einsum(
        "thd,hde->the", lin_query, carried, preferred_element_type=jnp.float32
    )
    local_scores = jnp.einsum(
        "thd,shd->hts", lin_query, lin_key, preferred_element_type=jnp.float32
    )
    causal = lax.iota(jnp.int32, row_count)[:, None] >= lax.iota(jnp.int32, row_count)[None, :]
    local_scores = jnp.where(causal[None], local_scores, 0.0).astype(jnp.bfloat16)
    mixed_rows = carried_part + jnp.einsum(
        "hts,she->the", local_scores, lin_value, preferred_element_type=jnp.float32
    )
    return rms_rows(mixed_rows).astype(jnp.bfloat16).reshape(row_count, head_width)


def solution(mesh):
    return jax.shard_map(
        body,
        mesh=mesh,
        in_specs=(
            P("ctx", None),
            P("ctx", "head"),
            P("ctx", "head"),
            P("ctx", "head"),
            P("head", None),
            P(None, "head"),
            P(None, "head"),
            P(None, "head"),
        ),
        out_specs=P("ctx", "head"),
        check_vma=False,
    )
```

profile of v0, /device:TPU:7, one launch (start us, length us, event | category | flops | bytes accessed | tf_op | source)
XLA Modules:
  0.0 547.1 jit_solution(11878632817526274923)
XLA Ops:
  8.7 0.9 copy_bitcast_fusion.1
  9.6 96.5 %all-gather.5.cloned.1.call-done = bf16[12288,128]{1,0:T(8,128)(2,1)} async-done(((bf16[192,128]{1,0:T(8,128)(2,1)}), bf16[12288,128]{1,0:T(8,128)(2,1)}) %all-gather.5.cloned.1.call-update) | async-done | bytes 3145744 | tf_op jit(solution)/shard_map/all_gather | solution.py:116
  106.2 90.8 %all-gather.7.cloned.1.call-done = bf16[12288,128]{1,0:T(8,128)(2,1)} async-done(((bf16[192,128]{1,0:T(8,128)(2,1)}), bf16[12288,128]{1,0:T(8,128)(2,1)}) %all-gather.7.cloned.1.call-update) | async-done | bytes 3145744 | tf_op jit(solution)/shard_map/all_gather | solution.py:117
  197.0 67.1 %while.33 = (s32[]{:T(128)}, f32[2,192]{1,0:T(2,128)S(1)}, f32[2,192]{1,0:T(2,128)S(1)}, f32[2,192,128]{2,1,0:T(8,128)S(1)}, s32[8]{0:T(128)S(1)}, /*index=5*/s3...) while((s32[]{:T(128)}, f32[2,192]{1,0:T(2,128)S(1)}, ...), condition=%wide.region_8.9_spmd.clone, body=%wide.region_0.8_spmd.clone.sunk | while | flops 307694016 | bytes 11148713 | solution.py:95
  197.0 1.2 dynamic-slice_bitcast_fusion.3
  200.8 4.3 conditional.3
  202.0 1.1 fusion.4
  203.8 1.3 fusion.8
  205.8 1.2 dynamic-slice_bitcast_fusion.3
  209.5 4.3 conditional.3
  210.7 1.1 fusion.4
  212.6 1.3 fusion.8
  214.5 1.2 dynamic-slice_bitcast_fusion.3
  218.3 4.3 conditional.3
  219.5 1.1 fusion.4
  221.3 1.3 fusion.8
  223.3 1.2 dynamic-slice_bitcast_fusion.3
  227.0 4.3 conditional.3
  228.2 1.1 fusion.4
  230.0 1.3 fusion.8
  232.0 1.2 dynamic-slice_bitcast_fusion.3
  235.8 4.3 conditional.3
  236.9 1.1 fusion.4
  238.8 1.3 fusion.8
  240.8 1.2 dynamic-slice_bitcast_fusion.3
  244.5 4.3 conditional.3
  245.7 1.1 fusion.4
  247.5 1.3 fusion.8
  249.5 1.2 dynamic-slice_bitcast_fusion.3
  253.2 5.1 conditional.3
  254.9 1.4 fusion.15
  257.0 1.4 fusion.21
  259.1 1.2 dynamic-slice_bitcast_fusion.3
  264.1 1.8 convolution_convert_fusion
  266.0 113.1 %all-reduce.2.cloned.1.call-done = bf16[192,4096]{1,0:T(8,128)(2,1)} async-done(((bf16[192,4096]{1,0:T(8,128)(2,1)}), bf16[192,4096]{1,0:T(8,128)(2,1)}) %all-reduce.2.cloned.1.call-update) | async-done | bytes 1572880 | tf_op jit(solution)/shard_map/psum | solution.py:125
  379.1 2.6 multiply_reduce_fusion
  382.5 1.0 copy-done.4
  384.1 1.5 copy-done.5
  387.2 2.6 fusion.32
  390.2 90.0 %all-gather.9.cloned.1.call-done = bf16[128,128,128]{2,1,0:T(8,128)(2,1)} async-done(((bf16[2,128,128]{2,1,0:T(8,128)(2,1)}), bf16[128,128,128]{2,1,0:T(8,128)(2,1)}) %all-gather.9.cloned.1.call-update) | async-done | bytes 4194320 | tf_op jit(solution)/shard_map/all_gather | solution.py:14
  480.2 59.3 %while.34 = (s32[]{:T(128)}, f32[2,128,128]{2,1,0:T(8,128)S(1)}, s32[]{:T(128)}, bf16[64,2,128,128]{3,2,1,0:T(8,128)(2,1)}, s32[]{:T(128)}, /*index=5*/s32[]{:T(128)}) while((s32[]{:T(128)}, f32[2,128,128]{2,1,0:T(8,128)S(1)}, s32[]{:T(128)}, bf16[64,2,128,128]{3,2,1,0:T(8,128)(2,1)}, s32[]{:T(128)}, ...), condition=%wide.region_12.13_spmd.clone, body=%wide.region_11.12_spmd.clone.sunk | while | flops 131076 | bytes 327773 | solution.py:22
  481.1 0.9 add_select_fusion.2
  482.0 0.9 add_select_fusion.2
  483.0 0.9 add_select_fusion.2
  483.9 0.9 add_select_fusion.2
  484.8 0.9 add_select_fusion.2
  485.7 0.9 add_select_fusion.2
  486.7 0.9 add_select_fusion.2
  487.6 0.9 add_select_fusion.2
  488.5 0.9 add_select_fusion.2
  489.4 0.9 add_select_fusion.2
  490.4 0.9 add_select_fusion.2
  491.3 0.9 add_select_fusion.2
  492.2 0.9 add_select_fusion.2
  496.9 0.9 add_select_fusion.2
  500.6 0.9 add_select_fusion.2
  505.2 0.9 add_select_fusion.2
  509.8 0.9 add_select_fusion.2
  514.5 0.9 add_select_fusion.2
  518.2 0.9 add_select_fusion.2
  522.8 0.9 add_select_fusion.2
  527.4 0.9 add_select_fusion.2
  532.1 0.9 add_select_fusion.2
  535.8 0.9 add_select_fusion.2
  (126 shorter events, 68.4 us)
Async XLA Ops:
  6.5 257.6 %copy-start = (bf16[256,4096]{1,0:T(8,128)(2,1)S(1)}, bf16[256,4096]{1,0:T(8,128)(2,1)}, u32[]{:S(2)}) copy-start(bf16[256,4096]{1,0:T(8,128)(2,1)} %param.19) | copy-start | bytes 6291460
  6.5 99.6 %all-gather.5.cloned.1.call-start = ((), (), s32[]{:S(2)}) async-start(), calls=%async_computation | async-start | bytes 3194880 | tf_op jit(solution)/shard_map/all_gather | solution.py:116
  7.3 189.7 %all-gather.7.cloned.1.call-start = ((), (), s32[]{:S(2)}) async-start(), calls=%async_computation.1 | async-start | bytes 3194880 | tf_op jit(solution)/shard_map/all_gather | solution.py:117
  8.0 371.1 %all-reduce.2.cloned.1.call-start = ((), (), s32[]{:S(2)}) async-start(), calls=%async_computation.2 | async-start | bytes 3145728 | tf_op jit(solution)/shard_map/psum | solution.py:125
  266.0 214.2 %all-gather.9.cloned.1.call-start = ((), (), s32[]{:S(2)}) async-start(), calls=%async_computation.3 | async-start | bytes 4259840 | tf_op jit(solution)/shard_map/all_gather | solution.py:14
  379.1 2.6 copy-start.1
  379.1 2.8 copy-start.2
  381.9 1.6 copy-start.4
  383.5 2.7 copy-start.3
  383.5 2.2 copy-start.5
Sparse Core Ops, SparseCore 0:
  11.3 94.8 all-gather.4
  110.1 86.8 all-gather.6
  266.1 112.9 all-reduce.1
  387.2 92.8 all-gather.8
where the time goes:
time: 554 us; the launch traced here: 547 us
  waiting for transfers between devices  392 us (71%)
  other arithmetic  79.4 us (14%)
  local copies, waits for them, and re-layouts  24.4 us (4%)
  matrix products  20.3 us (4%)
  loops' own time  17.7 us (3%)
  between operations  13.2 us (2%)
    psum x1, waiting for transfers between devices, body(): lax.psum(jnp.dot(attended, out_weight, preferred_element_type=jnp.float32...  113 us
    all_gather x1, waiting for transfers between devices, body(): lax.all_gather(key_soft, 'ctx', axis=0, tiled=True)  96.5 us
    all_gather x1, waiting for transfers between devices, body(): lax.all_gather(value_soft, 'ctx', axis=0, tiled=True)  90.8 us
    all_gather x1, waiting for transfers between devices, prefix(): everything = lax.all_gather(x.astype(jnp.bfloat16), axis)  90 us
    select_n x64, other arithmetic, lap(): return jnp.where(reached, new, before)  57.8 us
    another operation x1, loops' own time, fold_keys(): lax.scan(step_fn, carry, (key_blocks, value_blocks, jnp.arange(block_coun...  16.1 us
  transfers between devices with their start and end apart: 4, of which 4 were waited for; matrix products, arithmetic and copies ran while one was open for 1% of the time, Pallas kernels for 0%

commit v1 on v0

v1 whole, which is shorter than its diff:
```python
import math

import jax
import jax.numpy as jnp
from jax import lax
from jax.experimental import pallas as pl
from jax.experimental.pallas import tpu as pltpu
from jax.sharding import PartitionSpec as P

MESH = pl.DeviceIdType.MESH
HEAD = 128
TOK = 192
D = 4096
NX, NY, NZ = 4, 8, 12
SEG = 2 * NY
ROWS = TOK // NZ
PIECES = 4
WIDE = D // PIECES
QROWS = 2 * TOK
KROWS = 2 * TOK
C2 = math.log2(math.e) / math.sqrt(HEAD)
F32, BF16 = jnp.float32, jnp.bfloat16
NT = (((1,), (1,)), ((), ()))
TN = (((0,), (0,)), ((), ()))
DIST = (1, -1, 2, -2, 3, -3, 4)


def chain(direction, piece):
    return 6 if (direction == 0) == (piece < PIECES // 2) else 5


def kernel(
    hidden, query, key, value, w_out, w_q, w_k, w_v, out,
    hid, wo, wq, wk, wv,
    qb, kb, vb, vt, acc, stat, ob, mlb, po, pml, att,
    branch, rs_send, rs_recv, normed, proj,
    state, r1, tot, r2, ret, r3, keypad, mixed, before,
    load_sem,
    kv_ss, kv_rs, core_ss, core_rs, q_ss, q_rs, o_ss, o_rs,
    rs_ss, rs_rs, ag_ss, ag_rs, p1_ss, p1_rs, p2_ss, p2_rs, p3_ss, p3_rs,
):
    c = lax.axis_index("ctx")
    z = lax.axis_index("head")
    x, seg = c // SEG, c % SEG
    y, core = seg // 2, seg % 2

    def dev(xx, ss):
        return {"ctx": xx * SEG + ss, "head": z}

    def zdev(step):
        return {"ctx": c, "head": (z + step + NZ) % NZ}

    def ydev(step):
        return dev(x, ((y + step + NY) % NY) * 2 + core)

    partner = dev(x, y * 2 + (1 - core))

    def remote(src, dst, send, recv, to):
        return pltpu.make_async_remote_copy(
            src_ref=src, dst_ref=dst, send_sem=send, recv_sem=recv, device_id=to, device_id_type=MESH
        )

    loads = [
        pltpu.make_async_copy(w_out, wo, load_sem.at[0]),
        pltpu.make_async_copy(hidden.at[pl.ds(pl.multiple_of(z * ROWS, ROWS), ROWS)], hid, load_sem.at[1]),
        pltpu.make_async_copy(w_k, wk, load_sem.at[2]),
        pltpu.make_async_copy(w_v, wv, load_sem.at[3]),
        pltpu.make_async_copy(w_q, wq, load_sem.at[4]),
    ]
    for load in loads:
        load.start()

    barrier = pltpu.get_barrier_semaphore()
    for o in range(1, SEG):
        pl.semaphore_signal(barrier, inc=1, device_id=dev(x, (seg + o) % SEG), device_id_type=MESH)
    for o in range(1, NX):
        pl.semaphore_signal(barrier, inc=1, device_id=dev((x + o) % NX, seg), device_id_type=MESH)
    for o in (1, -1):
        pl.semaphore_signal(barrier, inc=1, device_id=zdev(o), device_id_type=MESH)

    own_rows = pl.ds(pl.multiple_of(core * TOK, TOK), TOK)
    other_rows = pl.ds(pl.multiple_of((1 - core) * TOK, TOK), TOK)
    qb[0, pl.ds(0, TOK), :] = query[:, pl.ds(0, HEAD)]
    qb[0, pl.ds(TOK, TOK), :] = query[:, pl.ds(HEAD, HEAD)]
    kb[y, own_rows, :] = key[...]
    vb[y, own_rows, :] = value[...]
    acc[...] = jnp.zeros_like(acc)
    stat[...] = jnp.zeros_like(stat)
    stat[:, 0, :] = jnp.full((NX, QROWS), -1e30, F32)
    pl.semaphore_wait(barrier, SEG - 1 + NX - 1 + 2)

    def kv_copy(i, which):
        d = DIST[i]
        buf = (kb, vb)[which]
        if abs(d) <= 2:
            source, step = y, d
        elif abs(d) == 3:
            sign = 1 if d > 0 else -1
            source, step = (y - 2 * sign + NY) % NY, sign
        else:
            sign = 1 if which == 0 else -1
            source, step = (y - 2 * sign + NY) % NY, 2 * sign
        ref = buf.at[source, own_rows]
        return remote(ref, ref, kv_ss.at[i, which], kv_rs.at[i, which], ydev(step))

    def kv_arrival(i, which):
        ref = (kb, vb)[which].at[(y - DIST[i] + NY) % NY, own_rows]
        return remote(ref, ref, kv_ss.at[i, which], kv_rs.at[i, which], partner)

    def core_copy(i, which):
        d = 0 if i == 0 else DIST[i - 1]
        ref = (kb, vb)[which].at[(y - d + NY) % NY, own_rows]
        return remote(ref, ref, core_ss.at[i, which], core_rs.at[i, which], partner)

    def core_arrival(i, which):
        d = 0 if i == 0 else DIST[i - 1]
        ref = (kb, vb)[which].at[(y - d + NY) % NY, other_rows]
        return remote(ref, ref, core_ss.at[i, which], core_rs.at[i, which], partner)

    def q_copy(o):
        return remote(qb.at[0], qb.at[o], q_ss.at[o], q_rs.at[o], dev((x - o + NX) % NX, seg))

    def o_copies(o):
        to = dev((x + o) % NX, seg)
        return (
            remote(ob.at[o], po.at[o], o_ss.at[o, 0], o_rs.at[o, 0], to),
            remote(mlb.at[o], pml.at[o], o_ss.at[o, 1], o_rs.at[o, 1], to),
        )

    for which in (0, 1):
        core_copy(0, which).start()
    for i in range(4):
        for which in (0, 1):
            kv_copy(i, which).start()
    for o in range(1, NX):
        @pl.when(x >= o)
        def _():
            q_copy(o).start()

    def unit(o, yk, masked):
        scores = lax.dot_general(kb[yk], qb[o], NT, preferred_element_type=F32)
        if masked:
            key_pos = lax.broadcasted_iota(jnp.int32, (KROWS, QROWS), 0)
            column = lax.broadcasted_iota(jnp.int32, (KROWS, QROWS), 1)
            query_pos = core * TOK + jnp.where(column >= TOK, column - TOK, column)
            scores = jnp.where(key_pos <= query_pos, scores, -1e30)
        old_max = stat[o, pl.ds(0, 1), :]
        new_max = jnp.maximum(old_max, jnp.max(scores, axis=0, keepdims=True))
        weights = jnp.exp2(scores * C2 - new_max * C2)
        factor = jnp.exp2((old_max - new_max) * C2)
        stat[o, pl.ds(0, 1), :] = new_max
        stat[o, pl.ds(1, 1), :] = stat[o, pl.ds(1, 1), :] * factor + jnp.sum(weights, axis=0, keepdims=True)
        acc[o] = acc[o] * factor + jnp.dot(vt[yk], weights.astype(BF16), preferred_element_type=F32)

    def turn_values(yk):
        vt[yk] = jnp.transpose(vb[yk].astype(F32)).astype(BF16)

    def later_units(yk):
        def step(o, carry):
            unit(o, yk, False)
            return carry

        lax.fori_loop(1, NX - x, step, 0)

    def group(first, stride, count):
        def step(e, carry):
            yk = (y + first + stride * e + 2 * NY) % NY
            turn_values(yk)

            @pl.when(yk < y)
            def _():
                unit(0, yk, False)

            later_units(yk)
            return carry

        lax.fori_loop(0, count, step, 0)

    for which in (0, 1):
        core_arrival(0, which).wait_recv()
    turn_values(y)
    unit(0, y, True)
    for o in range(1, NX):
        @pl.when(x + o < NX)
        def _():
            q_copy(o).wait_recv()
    later_units(y)

    def receive(indices, forwards):
        for i in indices:
            for which in (0, 1):
                kv_arrival(i, which).wait_recv()
                for j in forwards.get((i, which), ()):
                    kv_copy(j, which).start()
                core_copy(i + 1, which).start()
        for i in indices:
            for which in (0, 1):
                core_arrival(i + 1, which).wait_recv()

    receive((0, 1), {})
    group(-1, 2, 2)
    receive((2, 3), {(2, 0): (6, 4), (2, 1): (4,), (3, 0): (5,), (3, 1): (6, 5)})
    group(-2, 4, 2)
    receive((4, 5, 6), {})
    group(-3, -1, 3)

    for o in range(1, NX):
        @pl.when(x + o < NX)
        def _():
            ob[o] = acc[o].astype(BF16)
            mlb[o] = stat[o]
            for copy in o_copies(o):
                copy.start()

    loads[0].wait()

    for o in range(1, NX):
        @pl.when(x >= o)
        def _():
            for copy in o_copies(o):
                copy.wait_recv()
            old_max, part_max = stat[0, pl.ds(0, 1), :], pml[o, pl.ds(0, 1), :]
            new_max = jnp.maximum(old_max, part_max)
            factor = jnp.exp2((old_max - new_max) * C2)
            part_factor = jnp.exp2((part_max - new_max) * C2)
            stat[0, pl.ds(0, 1), :] = new_max
            stat[0, pl.ds(1, 1), :] = stat[0, pl.ds(1, 1), :] * factor + pml[o, pl.ds(1, 1), :] * part_factor
            acc[0] = acc[0] * factor + po[o].astype(F32) * part_factor

    attended = jnp.transpose(acc[0] / stat[0, pl.ds(1, 1), :])
    att[:, pl.ds(0, HEAD)] = attended[:TOK].astype(BF16)
    att[:, pl.ds(HEAD, HEAD)] = attended[TOK:].astype(BF16)

    def rs_copy(direction, step, piece):
        return remote(
            rs_send.at[direction, step, piece],
            rs_recv.at[direction, step, piece],
            rs_ss.at[direction, step, piece],
            rs_rs.at[direction, step, piece],
            zdev(-1 if direction == 0 else 1),
        )

    for step in range(6):
        for piece in range(PIECES):
            if step == 0:
                branch[:, :, pl.ds(piece * WIDE, WIDE)] = jnp.dot(
                    att[...], wo[:, pl.ds(piece * WIDE, WIDE)], preferred_element_type=F32
                ).reshape(NZ, ROWS, WIDE)
            for direction in (0, 1):
                length = chain(direction, piece)
                if step < length:
                    away = length - step
                    target = (z + (-away if direction == 0 else away) + NZ) % NZ
                    term = branch[target, :, pl.ds(piece * WIDE, WIDE)]
                    if step > 0:
                        rs_copy(direction, step - 1, piece).wait_recv()
                        term = term + rs_recv[direction, step - 1, piece].astype(F32)
                    rs_send[direction, step, piece] = term.astype(BF16)
                    rs_copy(direction, step, piece).start()

    loads[1].wait()
    square = jnp.zeros((ROWS, 1), F32)
    for piece in range(PIECES):
        columns = pl.ds(piece * WIDE, WIDE)
        total = branch[z, :, columns]
        for direction in (0, 1):
            last = chain(direction, piece) - 1
            rs_copy(direction, last, piece).wait_recv()
            total = total + rs_recv[direction, last, piece].astype(F32)
        total = total + hid[:, columns].astype(F32)
        branch[z, :, columns] = total
        square = square + jnp.sum(total * total, axis=1, keepdims=True)
    scale = lax.rsqrt(square * (1.0 / D) + 1e-6)

    def rows_of(step, direction):
        place = (z + (step if direction == 0 else -step) + NZ) % NZ
        return pl.ds(pl.multiple_of(place * ROWS, ROWS), ROWS)

    def ag_copy(direction, step, piece):
        ref = normed.at[rows_of(step, direction), pl.ds(piece * WIDE, WIDE)]
        return remote(
            ref, ref, ag_ss.at[direction, step, piece], ag_rs.at[direction, step, piece],
            zdev(-1 if direction == 0 else 1),
        )

    def ag_arrival(direction, step, piece):
        ref = normed.at[rows_of(step + 1, direction), pl.ds(piece * WIDE, WIDE)]
        return remote(
            ref, ref, ag_ss.at[direction, step, piece], ag_rs.at[direction, step, piece],
            zdev(-1 if direction == 0 else 1),
        )

    for piece in range(PIECES):
        columns = pl.ds(piece * WIDE, WIDE)
        normed[rows_of(0, 0), columns] = (branch[z, :, columns] * scale).astype(BF16)
        for direction in (0, 1):
            ag_copy(direction, 0, piece).start()
    for step in range(6):
        for piece in range(PIECES):
            for direction in (0, 1):
                length = chain(direction, piece)
                if step < length:
                    ag_arrival(direction, step, piece).wait_recv()
                    if step + 1 < length:
                        ag_copy(direction, step + 1, piece).start()

    for load in loads[2:]:
        load.wait()
    DEEP = 512

    def project(weight, slot):
        proj[slot] = jnp.zeros((TOK, 2 * HEAD), F32)

        def step(i, carry):
            deep = pl.ds(pl.multiple_of(i * DEEP, DEEP), DEEP)
            proj[slot] += jnp.dot(normed[:, deep], weight[deep, :], preferred_element_type=F32)
            return carry

        lax.fori_loop(0, D // DEEP, step, 0)

    project(wk, 1)
    project(wv, 2)

    keypad[...] = jnp.zeros_like(keypad)
    keypad[pl.ds(0, TOK), :] = proj[1].astype(BF16).astype(F32)
    for h in range(2):
        lanes = pl.ds(h * HEAD, HEAD)
        turned = jnp.transpose(keypad[:, lanes])[:, :TOK].astype(BF16)
        part = jnp.dot(turned, proj[2, :, lanes].astype(BF16), preferred_element_type=F32)
        state[pl.ds(h * (SEG // 2), SEG // 2)] = part.astype(BF16).reshape(SEG // 2, 16, HEAD)

    def p1_copy(o):
        return remote(state.at[(seg + o) % SEG], r1.at[seg], p1_ss.at[o], p1_rs.at[o], dev(x, (seg + o) % SEG))

    def p1_arrival(o):
        ref = r1.at[(seg - o + SEG) % SEG]
        return remote(ref, ref, p1_ss.at[o], p1_rs.at[o], partner)

    def p2_copy(o):
        return remote(tot, r2.at[o], p2_ss.at[o], p2_rs.at[o], dev((x + o) % NX, seg))

    def p3_copy(o):
        to = (seg + o) % SEG
        return remote(ret.at[to], r3.at[seg], p3_ss.at[o], p3_rs.at[o], dev(x, to))

    def p3_arrival(o):
        ref = r3.at[(seg - o + SEG) % SEG]
        return remote(ref, ref, p3_ss.at[o], p3_rs.at[o], partner)

    for o in range(1, SEG):
        p1_copy(o).start()
    r1[seg] = state[seg]
    project(wq, 0)
    for o in range(1, SEG):
        p1_arrival(o).wait_recv()
    run = jnp.zeros((16, HEAD), F32)
    for i in range(SEG):
        run = run + r1[i].astype(F32)
    tot[...] = run
    for o in range(1, NX):
        @pl.when(x + o < NX)
        def _():
            p2_copy(o).start()

    row = lax.broadcasted_iota(jnp.int32, (TOK, TOK), 0)
    column = lax.broadcasted_iota(jnp.int32, (TOK, TOK), 1)
    for h in range(2):
        lanes = pl.ds(h * HEAD, HEAD)
        near = lax.dot_general(
            proj[0, :, lanes].astype(BF16), proj[1, :, lanes].astype(BF16), NT, preferred_element_type=F32
        )
        near = jnp.where(row >= column, near, 0.0).astype(BF16)
        mixed[:, lanes] = jnp.dot(near, proj[2, :, lanes].astype(BF16), preferred_element_type=F32)

    before[...] = jnp.zeros_like(before)
    for o in range(1, NX):
        @pl.when(x >= o)
        def _():
            p2_copy(o).wait_recv()
            before[...] += r2[o]
    run = before[...]
    for i in range(SEG):
        ret[i] = run.astype(BF16)
        run = run + r1[i].astype(F32)
    for o in range(1, SEG):
        p3_copy(o).start()
    r3[seg] = ret[seg]
    for o in range(1, SEG):
        p3_arrival(o).wait_recv()

    for h in range(2):
        lanes = pl.ds(h * HEAD, HEAD)
        carried = r3[pl.ds(h * (SEG // 2), SEG // 2)].reshape(HEAD, HEAD)
        total = mixed[:, lanes] + jnp.dot(proj[0, :, lanes].astype(BF16), carried, preferred_element_type=F32)
        mean = jnp.mean(total * total, axis=1, keepdims=True)
        out[:, lanes] = (total * lax.rsqrt(mean + 1e-6)).astype(BF16)

    for which in (0, 1):
        for i in range(8):
            core_copy(i, which).wait_send()
        for i in range(7):
            kv_copy(i, which).wait_send()
    for o in range(1, NX):
        @pl.when(x >= o)
        def _():
            q_copy(o).wait_send()

        @pl.when(x + o < NX)
        def _():
            for copy in o_copies(o):
                copy.wait_send()
            p2_copy(o).wait_send()
    for direction in (0, 1):
        for piece in range(PIECES):
            for step in range(chain(direction, piece)):
                rs_copy(direction, step, piece).wait_send()
                ag_copy(direction, step, piece).wait_send()
    for o in range(1, SEG):
        p1_copy(o).wait_send()
        p3_copy(o).wait_send()


def body(*args):
    vmem = pl.BlockSpec(memory_space=pltpu.VMEM)
    anywhere = pl.BlockSpec(memory_space=pl.ANY)
    dma = pltpu.SemaphoreType.DMA
    scratch = [
        pltpu.VMEM((ROWS, D), BF16),
        pltpu.VMEM((2 * HEAD, D), BF16),
        pltpu.VMEM((D, 2 * HEAD), BF16),
        pltpu.VMEM((D, 2 * HEAD), BF16),
        pltpu.VMEM((D, 2 * HEAD), BF16),
        pltpu.VMEM((NX, QROWS, HEAD), BF16),
        pltpu.VMEM((NY, KROWS, HEAD), BF16),
        pltpu.VMEM((NY, KROWS, HEAD), BF16),
        pltpu.VMEM((NY, HEAD, KROWS), BF16),
        pltpu.VMEM((NX, HEAD, QROWS), F32),
        pltpu.VMEM((NX, 8, QROWS), F32),
        pltpu.VMEM((NX, HEAD, QROWS), BF16),
        pltpu.VMEM((NX, 8, QROWS), F32),
        pltpu.VMEM((NX, HEAD, QROWS), BF16),
        pltpu.VMEM((NX, 8, QROWS), F32),
        pltpu.VMEM((TOK, 2 * HEAD), BF16),
        pltpu.VMEM((NZ, ROWS, D), F32),
        pltpu.VMEM((2, 6, PIECES, ROWS, WIDE), BF16),
        pltpu.VMEM((2, 6, PIECES, ROWS, WIDE), BF16),
        pltpu.VMEM((TOK, D), BF16),
        pltpu.VMEM((3, TOK, 2 * HEAD), F32),
        pltpu.VMEM((SEG, 16, HEAD), BF16),
        pltpu.VMEM((SEG, 16, HEAD), BF16),
        pltpu.VMEM((16, HEAD), F32),
        pltpu.VMEM((NX, 16, HEAD), F32),
        pltpu.VMEM((SEG, 16, HEAD), BF16),
        pltpu.VMEM((SEG, 16, HEAD), BF16),
        pltpu.VMEM((2 * HEAD, 2 * HEAD), F32),
        pltpu.VMEM((TOK, 2 * HEAD), F32),
        pltpu.VMEM((16, HEAD), F32),
        dma((5,)),
        dma((7, 2)),
        dma((7, 2)),
        dma((8, 2)),
        dma((8, 2)),
        dma((NX,)),
        dma((NX,)),
        dma((NX, 2)),
        dma((NX, 2)),
        dma((2, 6, PIECES)),
        dma((2, 6, PIECES)),
        dma((2, 6, PIECES)),
        dma((2, 6, PIECES)),
        dma((SEG,)),
        dma((SEG,)),
        dma((NX,)),
        dma((NX,)),
        dma((SEG,)),
        dma((SEG,)),
    ]
    return pl.pallas_call(
        kernel,
        out_shape=jax.ShapeDtypeStruct((TOK, 2 * HEAD), BF16),
        in_specs=[anywhere, vmem, vmem, vmem, anywhere, anywhere, anywhere, anywhere],
        out_specs=vmem,
        scratch_shapes=scratch,
        compiler_params=pltpu.CompilerParams(
            collective_id=0, has_side_effects=True, vmem_limit_bytes=48 * 1024 * 1024
        ),
    )(*args)


def solution(mesh):
    return jax.shard_map(
        body,
        mesh=mesh,
        in_specs=(
            P("ctx", None),
            P("ctx", "head"),
            P("ctx", "head"),
            P("ctx", "head"),
            P("head", None),
            P(None, "head"),
            P(None, "head"),
            P(None, "head"),
        ),
        out_specs=P("ctx", "head"),
        check_vma=False,
    )
```

time: 554 us -> 126 us (0.23); the launches traced: 547 us -> 126 us
  waiting for transfers between devices: 392 us -> 0 us
  Pallas kernels: 0 us -> 118 us
  other arithmetic: 79.4 us -> 0 us
  matrix products: 20.3 us -> 0 us
  loops' own time: 17.7 us -> 0 us
  local copies, waits for them, and re-layouts: 24.4 us -> 7.72 us
  between operations: 13.2 us -> 0.02 us
    all_gather x3 -> x0, waiting for transfers between devices: 277 us -> none  [the longest x1 96.5 us: body(): lax.all_gather(key_soft, 'ctx', axis=0, tiled=True)]
    pallas_call x0 -> x1, Pallas kernels: none -> 118 us  [body(): pl.pallas_call(kernel, out_shape=jax.ShapeDtypeStruct((TOK, 2 * HEAD), BF...]
    psum x1 -> x0, waiting for transfers between devices: 113 us -> none  [body(): lax.psum(jnp.dot(attended, out_weight, preferred_element_type=jnp.float32...]
    select_n x64 -> x0, other arithmetic: 57.8 us -> none  [lap(): return jnp.where(reached, new, before)]
    dot_general x21 -> x0, matrix products: 20.3 us -> none  [the longest x7 8.99 us: attend_block(): jnp.einsum('hqk,kd->hqd', weights.astype(jnp.bfloat16), value_rows, prefe...]
    another operation x10 -> x0, loops' own time: 17.7 us -> none  [the longest x1 16.1 us: fold_keys(): lax.scan(step_fn, carry, (key_blocks, value_blocks, jnp.arange(block_coun...]
    reduce_sum x8 -> x0, other arithmetic: 10.9 us -> none  [the longest x7 8.25 us: attend_block(): run_sum = run_sum * factor + jnp.sum(weights, axis=-1)]
    squeeze x8 -> x0, local copies, waits for them, and re-layouts: 9.33 us -> none  [fold_keys(): lax.scan(step_fn, carry, (key_blocks, value_blocks, jnp.arange(block_coun...]
  transfers between devices with their start and end apart: 4 -> 0, of which waited for: 4 -> 0; matrix products, arithmetic and copies ran while one was open for 1% -> 0% of each run, Pallas kernels for 0% -> 0%
where the time goes in v1:
time: 126 us
  Pallas kernels  118 us (94%)
  local copies, waits for them, and re-layouts  7.72 us (6%)
    pallas_call x1, Pallas kernels, body(): pl.pallas_call(kernel, out_shape=jax.ShapeDtypeStruct((TOK, 2 * HEAD), BF...  118 us
    unnamed x13, local copies, waits for them, and re-layouts  7.72 us

profile of v1, /device:TPU:7, one launch (start us, length us, event | category | flops | bytes accessed | tf_op | source)
XLA Modules:
  0.0 126.0 jit_solution(14628806473963869672)
XLA Ops:
  0.0 0.0 copy-start
  0.0 1.6 %copy-done = bf16[256,4096]{1,0:T(8,128)(2,1)S(1)} copy-done((bf16[256,4096]{1,0:T(8,128)(2,1)S(1)}, bf16[256,4096]{1,0:T(8,128)(2,1)}, u32[]{:S(2)}) %copy-start) | copy-done | bytes 2097176
  1.6 0.0 copy-start.1
  1.6 1.6 %copy-done.1 = bf16[4096,256]{1,0:T(8,128)(2,1)S(1)} copy-done((bf16[4096,256]{1,0:T(8,128)(2,1)S(1)}, bf16[4096,256]{1,0:T(8,128)(2,1)}, u32[]{:S(2)}) %copy-start.1) | copy-done | bytes 2097176
  3.2 0.0 copy-start.2
  3.2 1.4 %copy-done.2 = bf16[192,4096]{1,0:T(8,128)(2,1)S(1)} copy-done((bf16[192,4096]{1,0:T(8,128)(2,1)S(1)}, bf16[192,4096]{1,0:T(8,128)(2,1)}, u32[]{:S(2)}) %copy-start.2) | copy-done | bytes 1572888
  4.6 0.0 copy-start.3
  4.6 0.9 copy-done.3
  5.5 0.0 copy-start.4
  5.5 0.8 copy-done.4
  6.3 0.0 copy-start.5
  6.3 0.8 copy-done.5
  7.1 118.3 %shard_map.82 = bf16[192,256]{1,0:T(8,128)(2,1)S(1)} custom-call(bf16[192,4096]{1,0:T(8,128)(2,1)S(1)} %copy-done.2, bf16[192,256]{1,0:T(8,128)(2,1)S(1)} %copy-done.3, bf16[192,128]{1,0:T(8,128)(2,1)S(1)} %copy-done.4, bf16[192,128]{1,0:T(8,128)(2,1)S(1)} %copy-done.5, bf16[256,4096]{1,0:T(8,128)(2,1)S(1)} %copy-done, bf16[4096,256]{1,0:T(8,128)(2,1)S(1)} %copy-done.1, ...), custom_call_target="tpu_custom_call" | custom-call | tf_op jit(solution)/shard_map/pallas_call | solution.py:478
  125.4 0.6 copy.10
Async XLA Ops:
  0.0 1.6 %copy-start = (bf16[256,4096]{1,0:T(8,128)(2,1)S(1)}, bf16[256,4096]{1,0:T(8,128)(2,1)}, u32[]{:S(2)}) copy-start(bf16[256,4096]{1,0:T(8,128)(2,1)} %w_out.1) | copy-start | bytes 6291460
  1.6 1.6 %copy-start.1 = (bf16[4096,256]{1,0:T(8,128)(2,1)S(1)}, bf16[4096,256]{1,0:T(8,128)(2,1)}, u32[]{:S(2)}) copy-start(bf16[4096,256]{1,0:T(8,128)(2,1)} %w_q.1) | copy-start | bytes 6291460
  3.2 1.4 %copy-start.2 = (bf16[192,4096]{1,0:T(8,128)(2,1)S(1)}, bf16[192,4096]{1,0:T(8,128)(2,1)}, u32[]{:S(2)}) copy-start(bf16[192,4096]{1,0:T(8,128)(2,1)} %hidden.1) | copy-start | bytes 4718596
  4.6 0.9 copy-start.3
  5.5 0.8 copy-start.4
  6.3 0.8 copy-start.5

commit v2 on v1

--- a/solution.py
+++ b/solution.py
@@ -23,6 +23,7 @@
 NT = (((1,), (1,)), ((), ()))
 TN = (((0,), (0,)), ((), ()))
 DIST = (1, -1, 2, -2, 3, -3, 4)
+PAIRS = 4
 
 
 def chain(direction, piece):
@@ -32,7 +33,7 @@
 def kernel(
     hidden, query, key, value, w_out, w_q, w_k, w_v, out,
     hid, wo, wq, wk, wv,
-    qb, kb, vb, vt, acc, stat, ob, mlb, po, pml, att,
+    qin, qt, kb, vb, vt, acc, stat, ob, mlb, po, pml, att,
     branch, rs_send, rs_recv, normed, proj,
     state, r1, tot, r2, ret, r3, keypad, mixed, before,
     load_sem,
@@ -60,6 +61,10 @@
             src_ref=src, dst_ref=dst, send_sem=send, recv_sem=recv, device_id=to, device_id_type=MESH
         )
 
+    def half(buf, pair, place, mine=True):
+        start = place * KROWS + (core if mine else 1 - core) * TOK
+        return buf.at[pair, pl.ds(pl.multiple_of(start, TOK), TOK)]
+
     loads = [
         pltpu.make_async_copy(w_out, wo, load_sem.at[0]),
         pltpu.make_async_copy(hidden.at[pl.ds(pl.multiple_of(z * ROWS, ROWS), ROWS)], hid, load_sem.at[1]),
@@ -67,7 +72,12 @@
         pltpu.make_async_copy(w_v, wv, load_sem.at[3]),
         pltpu.make_async_copy(w_q, wq, load_sem.at[4]),
     ]
-    for load in loads:
+    first_loads = [
+        pltpu.make_async_copy(query, qin, load_sem.at[5]),
+        pltpu.make_async_copy(key, half(kb, PAIRS - 1, 0), load_sem.at[6]),
+        pltpu.make_async_copy(value, half(vb, PAIRS - 1, 0), load_sem.at[7]),
+    ]
+    for load in first_loads:
         load.start()
 
     barrier = pltpu.get_barrier_semaphore()
@@ -78,47 +88,37 @@
     for o in (1, -1):
         pl.semaphore_signal(barrier, inc=1, device_id=zdev(o), device_id_type=MESH)
 
-    own_rows = pl.ds(pl.multiple_of(core * TOK, TOK), TOK)
-    other_rows = pl.ds(pl.multiple_of((1 - core) * TOK, TOK), TOK)
-    qb[0, pl.ds(0, TOK), :] = query[:, pl.ds(0, HEAD)]
-    qb[0, pl.ds(TOK, TOK), :] = query[:, pl.ds(HEAD, HEAD)]
-    kb[y, own_rows, :] = key[...]
-    vb[y, own_rows, :] = value[...]
-    acc[...] = jnp.zeros_like(acc)
-    stat[...] = jnp.zeros_like(stat)
-    stat[:, 0, :] = jnp.full((NX, QROWS), -1e30, F32)
+    for load in first_loads:
+        load.wait()
+    stacked = jnp.concatenate([qin[:, pl.ds(0, HEAD)], qin[:, pl.ds(HEAD, HEAD)]], axis=0)
+    qt[0] = jnp.transpose(stacked.astype(F32)).astype(BF16)
     pl.semaphore_wait(barrier, SEG - 1 + NX - 1 + 2)
 
     def kv_copy(i, which):
-        d = DIST[i]
         buf = (kb, vb)[which]
-        if abs(d) <= 2:
-            source, step = y, d
-        elif abs(d) == 3:
-            sign = 1 if d > 0 else -1
-            source, step = (y - 2 * sign + NY) % NY, sign
+        if i < 4:
+            source, step = half(buf, PAIRS - 1, 0), DIST[i]
+        elif i < 6:
+            source, step = half(buf, 1, i - 4), (1, -1)[i - 4]
         else:
-            sign = 1 if which == 0 else -1
-            source, step = (y - 2 * sign + NY) % NY, 2 * sign
-        ref = buf.at[source, own_rows]
-        return remote(ref, ref, kv_ss.at[i, which], kv_rs.at[i, which], ydev(step))
-
-    def kv_arrival(i, which):
-        ref = (kb, vb)[which].at[(y - DIST[i] + NY) % NY, own_rows]
+            source, step = half(buf, 1, which), (2, -2)[which]
+        target = half(buf, i // 2, i % 2 if i < 6 else 1)
+        return remote(source, target, kv_ss.at[i, which], kv_rs.at[i, which], ydev(step))
+
+    def kv_arrival(i, pair, place, which):
+        ref = half((kb, vb)[which], pair, place)
         return remote(ref, ref, kv_ss.at[i, which], kv_rs.at[i, which], partner)
 
-    def core_copy(i, which):
-        d = 0 if i == 0 else DIST[i - 1]
-        ref = (kb, vb)[which].at[(y - d + NY) % NY, own_rows]
+    def core_copy(i, pair, place, which):
+        ref = half((kb, vb)[which], pair, place)
         return remote(ref, ref, core_ss.at[i, which], core_rs.at[i, which], partner)
 
-    def core_arrival(i, which):
-        d = 0 if i == 0 else DIST[i - 1]
-        ref = (kb, vb)[which].at[(y - d + NY) % NY, other_rows]
+    def core_arrival(i, pair, place, which):
+        ref = half((kb, vb)[which], pair, place, False)
         return remote(ref, ref, core_ss.at[i, which], core_rs.at[i, which], partner)
 
     def q_copy(o):
-        return remote(qb.at[0], qb.at[o], q_ss.at[o], q_rs.at[o], dev((x - o + NX) % NX, seg))
+        return remote(qt.at[0], qt.at[o], q_ss.at[o], q_rs.at[o], dev((x - o + NX) % NX, seg))
 
     def o_copies(o):
         to = dev((x + o) % NX, seg)
@@ -127,82 +127,92 @@
             remote(mlb.at[o], pml.at[o], o_ss.at[o, 1], o_rs.at[o, 1], to),
         )
 
-    for which in (0, 1):
-        core_copy(0, which).start()
-    for i in range(4):
+    for i in (2, 3, 0, 1):
         for which in (0, 1):
             kv_copy(i, which).start()
+    for which in (0, 1):
+        core_copy(7, PAIRS - 1, 0, which).start()
     for o in range(1, NX):
         @pl.when(x >= o)
         def _():
             q_copy(o).start()
-
-    def unit(o, yk, masked):
-        scores = lax.dot_general(kb[yk], qb[o], NT, preferred_element_type=F32)
-        if masked:
-            key_pos = lax.broadcasted_iota(jnp.int32, (KROWS, QROWS), 0)
-            column = lax.broadcasted_iota(jnp.int32, (KROWS, QROWS), 1)
-            query_pos = core * TOK + jnp.where(column >= TOK, column - TOK, column)
-            scores = jnp.where(key_pos <= query_pos, scores, -1e30)
+    for load in loads:
+        load.start()
+
+    def fold(o, scores, values):
         old_max = stat[o, pl.ds(0, 1), :]
-        new_max = jnp.maximum(old_max, jnp.max(scores, axis=0, keepdims=True))
-        weights = jnp.exp2(scores * C2 - new_max * C2)
-        factor = jnp.exp2((old_max - new_max) * C2)
+        new_max = jnp.maximum(old_max, jnp.max(scores, axis=0, keepdims=True) * C2)
+        weights = jnp.exp2(scores * C2 - new_max)
+        factor = jnp.exp2(old_max - new_max)
         stat[o, pl.ds(0, 1), :] = new_max
         stat[o, pl.ds(1, 1), :] = stat[o, pl.ds(1, 1), :] * factor + jnp.sum(weights, axis=0, keepdims=True)
-        acc[o] = acc[o] * factor + jnp.dot(vt[yk], weights.astype(BF16), preferred_element_type=F32)
-
-    def turn_values(yk):
-        vt[yk] = jnp.transpose(vb[yk].astype(F32)).astype(BF16)
-
-    def later_units(yk):
-        def step(o, carry):
-            unit(o, yk, False)
-            return carry
-
-        lax.fori_loop(1, NX - x, step, 0)
-
-    def group(first, stride, count):
-        def step(e, carry):
-            yk = (y + first + stride * e + 2 * NY) % NY
-            turn_values(yk)
-
-            @pl.when(yk < y)
+        acc[o] = acc[o] * factor + jnp.dot(values, weights.astype(BF16), preferred_element_type=F32)
+
+    def turn_values(pair, place):
+        rows = pl.ds(place * KROWS, KROWS)
+        vt[pair, :, rows] = jnp.transpose(vb[pair, rows, :].astype(F32)).astype(BF16)
+
+    acc[...] = jnp.zeros_like(acc)
+    stat[...] = jnp.zeros_like(stat)
+    stat[:, 0, :] = jnp.full((NX, QROWS), -1e30, F32)
+    for which in (0, 1):
+        core_arrival(7, PAIRS - 1, 0, which).wait_recv()
+    turn_values(PAIRS - 1, 0)
+    key_pos = lax.broadcasted_iota(jnp.int32, (KROWS, QROWS), 0)
+    column = lax.broadcasted_iota(jnp.int32, (KROWS, QROWS), 1)
+    query_pos = core * TOK + jnp.where(column >= TOK, column - TOK, column)
+    own = jnp.dot(kb[PAIRS - 1, pl.ds(0, KROWS), :], qt[0], preferred_element_type=F32)
+    fold(0, jnp.where(key_pos <= query_pos, own, -1e30), vt[PAIRS - 1, :, pl.ds(0, KROWS)])
+    for o in range(1, NX):
+        @pl.when(x + o < NX)
+        def _():
+            q_copy(o).wait_recv()
+
+    def pair_step(pair, carry):
+        @pl.when(pair < PAIRS - 1)
+        def _():
+            for place in (0, 1):
+                for which in (0, 1):
+                    i = 2 * pair + place
+                    kv_arrival(i, pair, place, which).wait_recv()
+
+                    @pl.when(pair == 1)
+                    def _():
+                        for j, w in {(0, 0): ((6, 0), (4, 0)), (0, 1): ((4, 1),), (1, 0): ((5, 0),), (1, 1): ((6, 1), (5, 1))}[place, which]:
+                            kv_copy(j, w).start()
+
+                    core_copy(i, pair, place, which).start()
+            for place in (0, 1):
+                for which in (0, 1):
+                    core_arrival(2 * pair + place, pair, place, which).wait_recv()
+            turn_values(pair, 0)
+
+        @pl.when(pair == PAIRS - 1)
+        def _():
+            for which in (0, 1):
+                kv_arrival(6, PAIRS - 1, 1, which).wait_recv()
+                core_copy(6, PAIRS - 1, 1, which).start()
+            for which in (0, 1):
+                core_arrival(6, PAIRS - 1, 1, which).wait_recv()
+
+        turn_values(pair, 1)
+
+        last = pair == PAIRS - 1
+        away = pair + 1
+        seen_0 = jnp.logical_and(jnp.logical_not(last), y >= away)
+        seen_1 = jnp.where(last, y >= away, y + away >= NY)
+        bias_0 = jnp.where(seen_0, 0.0, -1e30).astype(F32)
+        bias_1 = jnp.where(seen_1, 0.0, -1e30).astype(F32)
+        for count in range(NX):
+            @pl.when(x == NX - 1 - count)
             def _():
-                unit(0, yk, False)
-
-            later_units(yk)
-            return carry
-
-        lax.fori_loop(0, count, step, 0)
-
-    for which in (0, 1):
-        core_arrival(0, which).wait_recv()
-    turn_values(y)
-    unit(0, y, True)
-    for o in range(1, NX):
-        @pl.when(x + o < NX)
-        def _():
-            q_copy(o).wait_recv()
-    later_units(y)
-
-    def receive(indices, forwards):
-        for i in indices:
-            for which in (0, 1):
-                kv_arrival(i, which).wait_recv()
-                for j in forwards.get((i, which), ()):
-                    kv_copy(j, which).start()
-                core_copy(i + 1, which).start()
-        for i in indices:
-            for which in (0, 1):
-                core_arrival(i + 1, which).wait_recv()
-
-    receive((0, 1), {})
-    group(-1, 2, 2)
-    receive((2, 3), {(2, 0): (6, 4), (2, 1): (4,), (3, 0): (5,), (3, 1): (6, 5)})
-    group(-2, 4, 2)
-    receive((4, 5, 6), {})
-    group(-3, -1, 3)
+                found = [jnp.dot(kb[pair], qt[o], preferred_element_type=F32) for o in range(count + 1)]
+                found[0] = jnp.concatenate([found[0][:KROWS] + bias_0, found[0][KROWS:] + bias_1], axis=0)
+                for o in range(count + 1):
+                    fold(o, found[o], vt[pair])
+        return carry
+
+    lax.fori_loop(0, PAIRS, pair_step, 0)
 
     for o in range(1, NX):
         @pl.when(x + o < NX)
@@ -221,8 +231,8 @@
                 copy.wait_recv()
             old_max, part_max = stat[0, pl.ds(0, 1), :], pml[o, pl.ds(0, 1), :]
             new_max = jnp.maximum(old_max, part_max)
-            factor = jnp.exp2((old_max - new_max) * C2)
-            part_factor = jnp.exp2((part_max - new_max) * C2)
+            factor = jnp.exp2(old_max - new_max)
+            part_factor = jnp.exp2(part_max - new_max)
             stat[0, pl.ds(0, 1), :] = new_max
             stat[0, pl.ds(1, 1), :] = stat[0, pl.ds(1, 1), :] * factor + pml[o, pl.ds(1, 1), :] * part_factor
             acc[0] = acc[0] * factor + po[o].astype(F32) * part_factor
@@ -258,20 +268,6 @@
                     rs_send[direction, step, piece] = term.astype(BF16)
                     rs_copy(direction, step, piece).start()
 
-    loads[1].wait()
-    square = jnp.zeros((ROWS, 1), F32)
-    for piece in range(PIECES):
-        columns = pl.ds(piece * WIDE, WIDE)
-        total = branch[z, :, columns]
-        for direction in (0, 1):
-            last = chain(direction, piece) - 1
-            rs_copy(direction, last, piece).wait_recv()
-            total = total + rs_recv[direction, last, piece].astype(F32)
-        total = total + hid[:, columns].astype(F32)
-        branch[z, :, columns] = total
-        square = square + jnp.sum(total * total, axis=1, keepdims=True)
-    scale = lax.rsqrt(square * (1.0 / D) + 1e-6)
-
     def rows_of(step, direction):
         place = (z + (step if direction == 0 else -step) + NZ) % NZ
         return pl.ds(pl.multiple_of(place * ROWS, ROWS), ROWS)
@@ -290,11 +286,26 @@
             zdev(-1 if direction == 0 else 1),
         )
 
+    loads[1].wait()
     for piece in range(PIECES):
         columns = pl.ds(piece * WIDE, WIDE)
-        normed[rows_of(0, 0), columns] = (branch[z, :, columns] * scale).astype(BF16)
+        total = branch[z, :, columns] + hid[:, columns].astype(F32)
+        for direction in (0, 1):
+            last = chain(direction, piece) - 1
+            rs_copy(direction, last, piece).wait_recv()
+            total = total + rs_recv[direction, last, piece].astype(F32)
+        normed[rows_of(0, 0), columns] = total.astype(BF16)
         for direction in (0, 1):
             ag_copy(direction, 0, piece).start()
+
+    def project(weight, slot, piece):
+        columns = pl.ds(piece * WIDE, WIDE)
+        proj[slot] += jnp.dot(normed[:, columns], weight[columns, :], preferred_element_type=F32)
+
+    for load in loads[2:]:
+        load.wait()
+    proj[...] = jnp.zeros_like(proj)
+    square = jnp.zeros((TOK, 1), F32)
     for step in range(6):
         for piece in range(PIECES):
             for direction in (0, 1):
@@ -303,23 +314,14 @@
                     ag_arrival(direction, step, piece).wait_recv()
                     if step + 1 < length:
                         ag_copy(direction, step + 1, piece).start()
-
-    for load in loads[2:]:
-        load.wait()
-    DEEP = 512
-
-    def project(weight, slot):
-        proj[slot] = jnp.zeros((TOK, 2 * HEAD), F32)
-
-        def step(i, carry):
-            deep = pl.ds(pl.multiple_of(i * DEEP, DEEP), DEEP)
-            proj[slot] += jnp.dot(normed[:, deep], weight[deep, :], preferred_element_type=F32)
-            return carry
-
-        lax.fori_loop(0, D // DEEP, step, 0)
-
-    project(wk, 1)
-    project(wv, 2)
+            if step == 5:
+                project(wk, 1, piece)
+                project(wv, 2, piece)
+                rows = normed[:, pl.ds(piece * WIDE, WIDE)].astype(F32)
+                square = square + jnp.sum(rows * rows, axis=1, keepdims=True)
+    scale = lax.rsqrt(square * (1.0 / D) + 1e-6)
+    for slot in (1, 2):
+        proj[slot] = proj[slot] * scale
 
     keypad[...] = jnp.zeros_like(keypad)
     keypad[pl.ds(0, TOK), :] = proj[1].astype(BF16).astype(F32)
@@ -350,7 +352,9 @@
     for o in range(1, SEG):
         p1_copy(o).start()
     r1[seg] = state[seg]
-    project(wq, 0)
+    for piece in range(PIECES):
+        project(wq, 0, piece)
+    proj[0] = proj[0] * scale
     for o in range(1, SEG):
         p1_arrival(o).wait_recv()
     run = jnp.zeros((16, HEAD), F32)
@@ -397,7 +401,7 @@
 
     for which in (0, 1):
         for i in range(8):
-            core_copy(i, which).wait_send()
+            core_copy(i, 0, 0, which).wait_send()
         for i in range(7):
             kv_copy(i, which).wait_send()
     for o in range(1, NX):
@@ -430,10 +434,11 @@
         pltpu.VMEM((D, 2 * HEAD), BF16),
         pltpu.VMEM((D, 2 * HEAD), BF16),
         pltpu.VMEM((D, 2 * HEAD), BF16),
-        pltpu.VMEM((NX, QROWS, HEAD), BF16),
-        pltpu.VMEM((NY, KROWS, HEAD), BF16),
-        pltpu.VMEM((NY, KROWS, HEAD), BF16),
-        pltpu.VMEM((NY, HEAD, KROWS), BF16),
+        pltpu.VMEM((TOK, 2 * HEAD), BF16),
+        pltpu.VMEM((NX, HEAD, QROWS), BF16),
+        pltpu.VMEM((PAIRS, 2 * KROWS, HEAD), BF16),
+        pltpu.VMEM((PAIRS, 2 * KROWS, HEAD), BF16),
+        pltpu.VMEM((PAIRS, HEAD, 2 * KROWS), BF16),
         pltpu.VMEM((NX, HEAD, QROWS), F32),
         pltpu.VMEM((NX, 8, QROWS), F32),
         pltpu.VMEM((NX, HEAD, QROWS), BF16),
@@ -455,7 +460,7 @@
         pltpu.VMEM((2 * HEAD, 2 * HEAD), F32),
         pltpu.VMEM((TOK, 2 * HEAD), F32),
         pltpu.VMEM((16, HEAD), F32),
-        dma((5,)),
+        dma((8,)),
         dma((7, 2)),
         dma((7, 2)),
         dma((8, 2)),
@@ -478,11 +483,11 @@
     return pl.pallas_call(
         kernel,
         out_shape=jax.ShapeDtypeStruct((TOK, 2 * HEAD), BF16),
-        in_specs=[anywhere, vmem, vmem, vmem, anywhere, anywhere, anywhere, anywhere],
+        in_specs=[anywhere] * 8,
         out_specs=vmem,
         scratch_shapes=scratch,
         compiler_params=pltpu.CompilerParams(
-            collective_id=0, has_side_effects=True, vmem_limit_bytes=48 * 1024 * 1024
+            collective_id=0, has_side_effects=True, vmem_limit_bytes=60 * 1024 * 1024
         ),
     )(*args)
 

time: 126 us -> 110 us (0.87)
  Pallas kernels: 118 us -> 109 us
  local copies, waits for them, and re-layouts: 7.72 us -> 1.54 us
    pallas_call x1, Pallas kernels: 118 us -> 109 us  [body(): pl.pallas_call(kernel, out_shape=jax.ShapeDtypeStruct((TOK, 2 * HEAD), BF...]
    unnamed x13 -> x1, local copies, waits for them, and re-layouts: 7.72 us -> 1.54 us
where the time goes in v2:
time: 110 us
  Pallas kernels  109 us (99%)
  local copies, waits for them, and re-layouts  1.54 us (1%)
    pallas_call x1, Pallas kernels, body(): pl.pallas_call(kernel, out_shape=jax.ShapeDtypeStruct((TOK, 2 * HEAD), BF...  109 us

profile of v2, /device:TPU:7, one launch (start us, length us, event | category | flops | bytes accessed | tf_op | source)
XLA Modules:
  0.0 110.2 jit_solution(6738044358593289089)
XLA Ops:
  0.0 108.6 %shard_map.82 = bf16[192,256]{1,0:T(8,128)(2,1)} custom-call(bf16[192,4096]{1,0:T(8,128)(2,1)} %hidden.1, bf16[192,256]{1,0:T(8,128)(2,1)} %query.1, bf16[192,128]{1,0:T(8,128)(2,1)} %key.1, bf16[192,128]{1,0:T(8,128)(2,1)} %value.1, bf16[256,4096]{1,0:T(8,128)(2,1)} %w_out.1, bf16[4096,256]{1,0:T(8,128)(2,1)} %w_q.1, bf16[4096,256]{1,0:T(8,128)(2,1)} %w_k.1, ...), custom_call_target="tpu_custom_call" | custom-call | tf_op jit(solution)/shard_map/pallas_call | solution.py:483
  108.6 1.5 %copy.10 = bf16[192,256]{1,0:T(8,128)(2,1)} copy(bf16[192,256]{1,0:T(8,128)(2,1)} %shard_map.82) | data formatting | bytes 196608

commit v3 on v2

--- a/solution.py
+++ b/solution.py
@@ -13,6 +13,7 @@
 D = 4096
 NX, NY, NZ = 4, 8, 12
 SEG = 2 * NY
+NPAIR = NZ // 2
 ROWS = TOK // NZ
 PIECES = 4
 WIDE = D // PIECES
@@ -26,8 +27,8 @@
 PAIRS = 4
 
 
-def chain(direction, piece):
-    return 6 if (direction == 0) == (piece < PIECES // 2) else 5
+def chain(direction, piece, far=6):
+    return far if (direction == 0) == (piece < PIECES // 2) else far - 1
 
 
 def kernel(
@@ -35,8 +36,8 @@
     hid, wo, wq, wk, wv,
     qin, qt, kb, vb, vt, acc, stat, ob, mlb, po, pml, att,
     branch, rs_send, rs_recv, normed, proj,
-    state, r1, tot, r2, ret, r3, keypad, mixed, before,
-    load_sem,
+    att_in, state, r1, tot, r2, ret, r3, keypad, mixed, before,
+    load_sem, w_ss, w_rs, a_ss, a_rs,
     kv_ss, kv_rs, core_ss, core_rs, q_ss, q_rs, o_ss, o_rs,
     rs_ss, rs_rs, ag_ss, ag_rs, p1_ss, p1_rs, p2_ss, p2_rs, p3_ss, p3_rs,
 ):
@@ -44,6 +45,7 @@
     z = lax.axis_index("head")
     x, seg = c // SEG, c % SEG
     y, core = seg // 2, seg % 2
+    zpair, parity = z // 2, z % 2
 
     def dev(xx, ss):
         return {"ctx": xx * SEG + ss, "head": z}
@@ -66,7 +68,7 @@
         return buf.at[pair, pl.ds(pl.multiple_of(start, TOK), TOK)]
 
     loads = [
-        pltpu.make_async_copy(w_out, wo, load_sem.at[0]),
+        pltpu.make_async_copy(w_out, wo.at[pl.ds(0, 2 * HEAD)], load_sem.at[0]),
         pltpu.make_async_copy(hidden.at[pl.ds(pl.multiple_of(z * ROWS, ROWS), ROWS)], hid, load_sem.at[1]),
         pltpu.make_async_copy(w_k, wk, load_sem.at[2]),
         pltpu.make_async_copy(w_v, wv, load_sem.at[3]),
@@ -77,7 +79,7 @@
         pltpu.make_async_copy(key, half(kb, PAIRS - 1, 0), load_sem.at[6]),
         pltpu.make_async_copy(value, half(vb, PAIRS - 1, 0), load_sem.at[7]),
     ]
-    for load in first_loads:
+    for load in (*first_loads, loads[0]):
         load.start()
 
     barrier = pltpu.get_barrier_semaphore()
@@ -85,14 +87,14 @@
         pl.semaphore_signal(barrier, inc=1, device_id=dev(x, (seg + o) % SEG), device_id_type=MESH)
     for o in range(1, NX):
         pl.semaphore_signal(barrier, inc=1, device_id=dev((x + o) % NX, seg), device_id_type=MESH)
-    for o in (1, -1):
+    for o in (1, -1, 2, -2):
         pl.semaphore_signal(barrier, inc=1, device_id=zdev(o), device_id_type=MESH)
 
     for load in first_loads:
         load.wait()
     stacked = jnp.concatenate([qin[:, pl.ds(0, HEAD)], qin[:, pl.ds(HEAD, HEAD)]], axis=0)
     qt[0] = jnp.transpose(stacked.astype(F32)).astype(BF16)
-    pl.semaphore_wait(barrier, SEG - 1 + NX - 1 + 2)
+    pl.semaphore_wait(barrier, SEG - 1 + NX - 1 + 4)
 
     def kv_copy(i, which):
         buf = (kb, vb)[which]
@@ -127,6 +129,12 @@
             remote(mlb.at[o], pml.at[o], o_ss.at[o, 1], o_rs.at[o, 1], to),
         )
 
+    given = wo.at[pl.ds(pl.multiple_of(core * HEAD, HEAD), HEAD)]
+    taken = wo.at[pl.ds(pl.multiple_of(2 * HEAD + core * HEAD, HEAD), HEAD)]
+    twin = {"ctx": c, "head": zpair * 2 + 1 - parity}
+    weight_copy = remote(given, taken, w_ss.at[0], w_rs.at[0], twin)
+    weight_share = remote(taken, taken, w_ss.at[1], w_rs.at[1], partner)
+
     for i in (2, 3, 0, 1):
         for which in (0, 1):
             kv_copy(i, which).start()
@@ -136,7 +144,9 @@
         @pl.when(x >= o)
         def _():
             q_copy(o).start()
-    for load in loads:
+    loads[0].wait()
+    weight_copy.start()
+    for load in loads[1:]:
         load.start()
 
     def fold(o, scores, values):
@@ -163,25 +173,31 @@
     query_pos = core * TOK + jnp.where(column >= TOK, column - TOK, column)
     own = jnp.dot(kb[PAIRS - 1, pl.ds(0, KROWS), :], qt[0], preferred_element_type=F32)
     fold(0, jnp.where(key_pos <= query_pos, own, -1e30), vt[PAIRS - 1, :, pl.ds(0, KROWS)])
+    forwards = {(2, 0): ((6, 0), (4, 0)), (2, 1): ((4, 1),), (3, 0): ((5, 0),), (3, 1): ((6, 1), (5, 1))}
+
+    def receive(i):
+        pair, place = (i // 2, i % 2) if i < 6 else (PAIRS - 1, 1)
+        for which in (0, 1):
+            kv_arrival(i, pair, place, which).wait_recv()
+            for j, w in forwards.get((i, which), ()):
+                kv_copy(j, w).start()
+            core_copy(i, pair, place, which).start()
+
+    for i in (2, 3, 0, 1):
+        receive(i)
     for o in range(1, NX):
         @pl.when(x + o < NX)
         def _():
             q_copy(o).wait_recv()
 
     def pair_step(pair, carry):
+        @pl.when(pair == 2)
+        def _():
+            for i in (4, 5, 6):
+                receive(i)
+
         @pl.when(pair < PAIRS - 1)
         def _():
-            for place in (0, 1):
-                for which in (0, 1):
-                    i = 2 * pair + place
-                    kv_arrival(i, pair, place, which).wait_recv()
-
-                    @pl.when(pair == 1)
-                    def _():
-                        for j, w in {(0, 0): ((6, 0), (4, 0)), (0, 1): ((4, 1),), (1, 0): ((5, 0),), (1, 1): ((6, 1), (5, 1))}[place, which]:
-                            kv_copy(j, w).start()
-
-                    core_copy(i, pair, place, which).start()
             for place in (0, 1):
                 for which in (0, 1):
                     core_arrival(2 * pair + place, pair, place, which).wait_recv()
@@ -189,9 +205,6 @@
 
         @pl.when(pair == PAIRS - 1)
         def _():
-            for which in (0, 1):
-                kv_arrival(6, PAIRS - 1, 1, which).wait_recv()
-                core_copy(6, PAIRS - 1, 1, which).start()
             for which in (0, 1):
                 core_arrival(6, PAIRS - 1, 1, which).wait_recv()
 
@@ -222,7 +235,8 @@
             for copy in o_copies(o):
                 copy.start()
 
-    loads[0].wait()
+    weight_copy.wait_recv()
+    weight_share.start()
 
     for o in range(1, NX):
         @pl.when(x >= o)
@@ -238,8 +252,26 @@
             acc[0] = acc[0] * factor + po[o].astype(F32) * part_factor
 
     attended = jnp.transpose(acc[0] / stat[0, pl.ds(1, 1), :])
-    att[:, pl.ds(0, HEAD)] = attended[:TOK].astype(BF16)
-    att[:, pl.ds(HEAD, HEAD)] = attended[TOK:].astype(BF16)
+    for chunk in range(NZ):
+        for h in range(2):
+            rows = attended[h * TOK + chunk * ROWS : h * TOK + (chunk + 1) * ROWS]
+            att[chunk % 2, chunk // 2, :, pl.ds(h * HEAD, HEAD)] = rows.astype(BF16)
+
+    att_copy = remote(att.at[1 - parity], att_in, a_ss.at[0], a_rs.at[0], twin)
+    att_copy.start()
+    branch[...] = jnp.zeros_like(branch)
+
+    def project_out(rows, depth_start, piece):
+        columns = pl.ds(piece * WIDE, WIDE)
+        term = jnp.dot(
+            rows.reshape(NPAIR * ROWS, 2 * HEAD), wo[pl.ds(depth_start, 2 * HEAD), columns], preferred_element_type=F32
+        )
+        branch[:, :, columns] += term.reshape(NPAIR, ROWS, WIDE)
+
+    for piece in range(PIECES):
+        project_out(att[parity], 0, piece)
+    weight_share.wait_recv()
+    att_copy.wait_recv()
 
     def rs_copy(direction, step, piece):
         return remote(
@@ -247,20 +279,18 @@
             rs_recv.at[direction, step, piece],
             rs_ss.at[direction, step, piece],
             rs_rs.at[direction, step, piece],
-            zdev(-1 if direction == 0 else 1),
-        )
-
-    for step in range(6):
+            zdev(-2 if direction == 0 else 2),
+        )
+
+    for step in range(3):
         for piece in range(PIECES):
             if step == 0:
-                branch[:, :, pl.ds(piece * WIDE, WIDE)] = jnp.dot(
-                    att[...], wo[:, pl.ds(piece * WIDE, WIDE)], preferred_element_type=F32
-                ).reshape(NZ, ROWS, WIDE)
+                project_out(att_in[...], 2 * HEAD, piece)
             for direction in (0, 1):
-                length = chain(direction, piece)
+                length = chain(direction, piece, 3)
                 if step < length:
                     away = length - step
-                    target = (z + (-away if direction == 0 else away) + NZ) % NZ
+                    target = (zpair + (-away if direction == 0 else away) + NPAIR) % NPAIR
                     term = branch[target, :, pl.ds(piece * WIDE, WIDE)]
                     if step > 0:
                         rs_copy(direction, step - 1, piece).wait_recv()
@@ -289,9 +319,9 @@
     loads[1].wait()
     for piece in range(PIECES):
         columns = pl.ds(piece * WIDE, WIDE)
-        total = branch[z, :, columns] + hid[:, columns].astype(F32)
+        total = branch[zpair, :, columns] + hid[:, columns].astype(F32)
         for direction in (0, 1):
-            last = chain(direction, piece) - 1
+            last = chain(direction, piece, 3) - 1
             rs_copy(direction, last, piece).wait_recv()
             total = total + rs_recv[direction, last, piece].astype(F32)
         normed[rows_of(0, 0), columns] = total.astype(BF16)
@@ -416,9 +446,13 @@
             p2_copy(o).wait_send()
     for direction in (0, 1):
         for piece in range(PIECES):
+            for step in range(chain(direction, piece, 3)):
+                rs_copy(direction, step, piece).wait_send()
             for step in range(chain(direction, piece)):
-                rs_copy(direction, step, piece).wait_send()
                 ag_copy(direction, step, piece).wait_send()
+    weight_copy.wait_send()
+    weight_share.wait_send()
+    att_copy.wait_send()
     for o in range(1, SEG):
         p1_copy(o).wait_send()
         p3_copy(o).wait_send()
@@ -430,7 +464,7 @@
     dma = pltpu.SemaphoreType.DMA
     scratch = [
         pltpu.VMEM((ROWS, D), BF16),
-        pltpu.VMEM((2 * HEAD, D), BF16),
+        pltpu.VMEM((4 * HEAD, D), BF16),
         pltpu.VMEM((D, 2 * HEAD), BF16),
         pltpu.VMEM((D, 2 * HEAD), BF16),
         pltpu.VMEM((D, 2 * HEAD), BF16),
@@ -445,12 +479,13 @@
         pltpu.VMEM((NX, 8, QROWS), F32),
         pltpu.VMEM((NX, HEAD, QROWS), BF16),
         pltpu.VMEM((NX, 8, QROWS), F32),
-        pltpu.VMEM((TOK, 2 * HEAD), BF16),
-        pltpu.VMEM((NZ, ROWS, D), F32),
-        pltpu.VMEM((2, 6, PIECES, ROWS, WIDE), BF16),
-        pltpu.VMEM((2, 6, PIECES, ROWS, WIDE), BF16),
+        pltpu.VMEM((2, NPAIR, ROWS, 2 * HEAD), BF16),
+        pltpu.VMEM((NPAIR, ROWS, D), F32),
+        pltpu.VMEM((2, 3, PIECES, ROWS, WIDE), BF16),
+        pltpu.VMEM((2, 3, PIECES, ROWS, WIDE), BF16),
         pltpu.VMEM((TOK, D), BF16),
         pltpu.VMEM((3, TOK, 2 * HEAD), F32),
+        pltpu.VMEM((NPAIR, ROWS, 2 * HEAD), BF16),
         pltpu.VMEM((SEG, 16, HEAD), BF16),
         pltpu.VMEM((SEG, 16, HEAD), BF16),
         pltpu.VMEM((16, HEAD), F32),
@@ -461,6 +496,10 @@
         pltpu.VMEM((TOK, 2 * HEAD), F32),
         pltpu.VMEM((16, HEAD), F32),
         dma((8,)),
+        dma((2,)),
+        dma((2,)),
+        dma((1,)),
+        dma((1,)),
         dma((7, 2)),
         dma((7, 2)),
         dma((8, 2)),
@@ -469,8 +508,8 @@
         dma((NX,)),
         dma((NX, 2)),
         dma((NX, 2)),
-        dma((2, 6, PIECES)),
-        dma((2, 6, PIECES)),
+        dma((2, 3, PIECES)),
+        dma((2, 3, PIECES)),
         dma((2, 6, PIECES)),
         dma((2, 6, PIECES)),
         dma((SEG,)),

time: 110 us -> 105 us (0.955)
  Pallas kernels: 109 us -> 104 us
    pallas_call x1, Pallas kernels: 109 us -> 104 us  [body(): pl.pallas_call(kernel, out_shape=jax.ShapeDtypeStruct((TOK, 2 * HEAD), BF...]
where the time goes in v3:
time: 105 us
  Pallas kernels  104 us (99%)
  local copies, waits for them, and re-layouts  1.54 us (1%)
    pallas_call x1, Pallas kernels, body(): pl.pallas_call(kernel, out_shape=jax.ShapeDtypeStruct((TOK, 2 * HEAD), BF...  104 us

profile of v3, /device:TPU:7, one launch (start us, length us, event | category | flops | bytes accessed | tf_op | source)
XLA Modules:
  0.0 105.3 jit_solution(2681514767550659465)
XLA Ops:
  0.0 103.7 %shard_map.82 = bf16[192,256]{1,0:T(8,128)(2,1)} custom-call(bf16[192,4096]{1,0:T(8,128)(2,1)} %hidden.1, bf16[192,256]{1,0:T(8,128)(2,1)} %query.1, bf16[192,128]{1,0:T(8,128)(2,1)} %key.1, bf16[192,128]{1,0:T(8,128)(2,1)} %value.1, bf16[256,4096]{1,0:T(8,128)(2,1)} %w_out.1, bf16[4096,256]{1,0:T(8,128)(2,1)} %w_q.1, bf16[4096,256]{1,0:T(8,128)(2,1)} %w_k.1, ...), custom_call_target="tpu_custom_call" | custom-call | tf_op jit(solution)/shard_map/pallas_call | solution.py:522
  103.7 1.5 %copy.10 = bf16[192,256]{1,0:T(8,128)(2,1)} copy(bf16[192,256]{1,0:T(8,128)(2,1)} %shard_map.82) | data formatting | bytes 196608

commit v4 on v3

--- a/solution.py
+++ b/solution.py
@@ -15,7 +15,7 @@
 SEG = 2 * NY
 NPAIR = NZ // 2
 ROWS = TOK // NZ
-PIECES = 4
+PIECES = 8
 WIDE = D // PIECES
 QROWS = 2 * TOK
 KROWS = 2 * TOK
@@ -25,6 +25,8 @@
 TN = (((0,), (0,)), ((), ()))
 DIST = (1, -1, 2, -2, 3, -3, 4)
 PAIRS = 4
+PARENT = {1: 0, 2: 1, 3: 2, 4: 2, 5: 4, 6: 4}
+FAR_FIRST = sorted(range(1, SEG), key=lambda o: -min(o, SEG - o))
 
 
 def chain(direction, piece, far=6):
@@ -259,17 +261,17 @@
 
     att_copy = remote(att.at[1 - parity], att_in, a_ss.at[0], a_rs.at[0], twin)
     att_copy.start()
-    branch[...] = jnp.zeros_like(branch)
 
     def project_out(rows, depth_start, piece):
         columns = pl.ds(piece * WIDE, WIDE)
         term = jnp.dot(
             rows.reshape(NPAIR * ROWS, 2 * HEAD), wo[pl.ds(depth_start, 2 * HEAD), columns], preferred_element_type=F32
         )
-        branch[:, :, columns] += term.reshape(NPAIR, ROWS, WIDE)
+        return columns, term.reshape(NPAIR, ROWS, WIDE)
 
     for piece in range(PIECES):
-        project_out(att[parity], 0, piece)
+        columns, term = project_out(att[parity], 0, piece)
+        branch[:, :, columns] = term
     weight_share.wait_recv()
     att_copy.wait_recv()
 
@@ -285,7 +287,8 @@
     for step in range(3):
         for piece in range(PIECES):
             if step == 0:
-                project_out(att_in[...], 2 * HEAD, piece)
+                columns, term = project_out(att_in[...], 2 * HEAD, piece)
+                branch[:, :, columns] += term
             for direction in (0, 1):
                 length = chain(direction, piece, 3)
                 if step < length:
@@ -298,23 +301,28 @@
                     rs_send[direction, step, piece] = term.astype(BF16)
                     rs_copy(direction, step, piece).start()
 
-    def rows_of(step, direction):
-        place = (z + (step if direction == 0 else -step) + NZ) % NZ
-        return pl.ds(pl.multiple_of(place * ROWS, ROWS), ROWS)
-
-    def ag_copy(direction, step, piece):
-        ref = normed.at[rows_of(step, direction), pl.ds(piece * WIDE, WIDE)]
+    def rows_of(direction, distance, piece):
+        place = (z + (distance if direction == 0 else -distance) + NZ) % NZ
+        rows = pl.ds(pl.multiple_of(place * ROWS, ROWS), ROWS)
+        return normed.at[rows, pl.ds(piece * WIDE, WIDE)]
+
+    def ag_remote(ref, direction, distance, piece, step):
         return remote(
-            ref, ref, ag_ss.at[direction, step, piece], ag_rs.at[direction, step, piece],
-            zdev(-1 if direction == 0 else 1),
+            ref, ref, ag_ss.at[direction, distance - 1, piece], ag_rs.at[direction, distance - 1, piece],
+            zdev(-step if direction == 0 else step),
         )
 
-    def ag_arrival(direction, step, piece):
-        ref = normed.at[rows_of(step + 1, direction), pl.ds(piece * WIDE, WIDE)]
-        return remote(
-            ref, ref, ag_ss.at[direction, step, piece], ag_rs.at[direction, step, piece],
-            zdev(-1 if direction == 0 else 1),
-        )
+    def ag_copy(direction, distance, piece):
+        parent = PARENT[distance]
+        return ag_remote(rows_of(direction, parent, piece), direction, distance, piece, distance - parent)
+
+    def ag_arrival(direction, distance, piece):
+        return ag_remote(rows_of(direction, distance, piece), direction, distance, piece, 1)
+
+    def pass_on(direction, distance, piece):
+        for farther in (6, 5, 4, 3, 2, 1):
+            if PARENT[farther] == distance and farther <= chain(direction, piece):
+                ag_copy(direction, farther, piece).start()
 
     loads[1].wait()
     for piece in range(PIECES):
@@ -324,9 +332,9 @@
             last = chain(direction, piece, 3) - 1
             rs_copy(direction, last, piece).wait_recv()
             total = total + rs_recv[direction, last, piece].astype(F32)
-        normed[rows_of(0, 0), columns] = total.astype(BF16)
+        normed[pl.ds(pl.multiple_of(z * ROWS, ROWS), ROWS), columns] = total.astype(BF16)
         for direction in (0, 1):
-            ag_copy(direction, 0, piece).start()
+            pass_on(direction, 0, piece)
 
     def project(weight, slot, piece):
         columns = pl.ds(piece * WIDE, WIDE)
@@ -336,15 +344,13 @@
         load.wait()
     proj[...] = jnp.zeros_like(proj)
     square = jnp.zeros((TOK, 1), F32)
-    for step in range(6):
+    for distance in (1, 2, 4, 3, 6, 5):
         for piece in range(PIECES):
             for direction in (0, 1):
-                length = chain(direction, piece)
-                if step < length:
-                    ag_arrival(direction, step, piece).wait_recv()
-                    if step + 1 < length:
-                        ag_copy(direction, step + 1, piece).start()
-            if step == 5:
+                if distance <= chain(direction, piece):
+                    ag_arrival(direction, distance, piece).wait_recv()
+                    pass_on(direction, distance, piece)
+            if distance == 5:
                 project(wk, 1, piece)
                 project(wv, 2, piece)
                 rows = normed[:, pl.ds(piece * WIDE, WIDE)].astype(F32)
@@ -379,7 +385,7 @@
         ref = r3.at[(seg - o + SEG) % SEG]
         return remote(ref, ref, p3_ss.at[o], p3_rs.at[o], partner)
 
-    for o in range(1, SEG):
+    for o in FAR_FIRST:
         p1_copy(o).start()
     r1[seg] = state[seg]
     for piece in range(PIECES):
@@ -416,7 +422,7 @@
     for i in range(SEG):
         ret[i] = run.astype(BF16)
         run = run + r1[i].astype(F32)
-    for o in range(1, SEG):
+    for o in FAR_FIRST:
         p3_copy(o).start()
     r3[seg] = ret[seg]
     for o in range(1, SEG):
@@ -448,8 +454,8 @@
         for piece in range(PIECES):
             for step in range(chain(direction, piece, 3)):
                 rs_copy(direction, step, piece).wait_send()
-            for step in range(chain(direction, piece)):
-                ag_copy(direction, step, piece).wait_send()
+            for distance in range(1, chain(direction, piece) + 1):
+                ag_copy(direction, distance, piece).wait_send()
     weight_copy.wait_send()
     weight_share.wait_send()
     att_copy.wait_send()

time: 105 us -> 104 us (level)
  no operation moved by 1% of the time
where the time goes in v4:
time: 104 us
  Pallas kernels  103 us (99%)
  local copies, waits for them, and re-layouts  1.54 us (1%)
    pallas_call x1, Pallas kernels, body(): pl.pallas_call(kernel, out_shape=jax.ShapeDtypeStruct((TOK, 2 * HEAD), BF...  103 us

profile of v4, /device:TPU:7, one launch (start us, length us, event | category | flops | bytes accessed | tf_op | source)
XLA Modules:
  0.0 104.2 jit_solution(7344787361075627346)
XLA Ops:
  0.0 102.7 %shard_map.82 = bf16[192,256]{1,0:T(8,128)(2,1)} custom-call(bf16[192,4096]{1,0:T(8,128)(2,1)} %hidden.1, bf16[192,256]{1,0:T(8,128)(2,1)} %query.1, bf16[192,128]{1,0:T(8,128)(2,1)} %key.1, bf16[192,128]{1,0:T(8,128)(2,1)} %value.1, bf16[256,4096]{1,0:T(8,128)(2,1)} %w_out.1, bf16[4096,256]{1,0:T(8,128)(2,1)} %w_q.1, bf16[4096,256]{1,0:T(8,128)(2,1)} %w_k.1, ...), custom_call_target="tpu_custom_call" | custom-call | tf_op jit(solution)/shard_map/pallas_call | solution.py:528
  102.7 1.5 %copy.10 = bf16[192,256]{1,0:T(8,128)(2,1)} copy(bf16[192,256]{1,0:T(8,128)(2,1)} %shard_map.82) | data formatting | bytes 196608

commit v5 on v4

--- a/solution.py
+++ b/solution.py
@@ -15,7 +15,7 @@
 SEG = 2 * NY
 NPAIR = NZ // 2
 ROWS = TOK // NZ
-PIECES = 8
+PIECES = 4
 WIDE = D // PIECES
 QROWS = 2 * TOK
 KROWS = 2 * TOK
@@ -254,13 +254,16 @@
             acc[0] = acc[0] * factor + po[o].astype(F32) * part_factor
 
     attended = jnp.transpose(acc[0] / stat[0, pl.ds(1, 1), :])
-    for chunk in range(NZ):
-        for h in range(2):
-            rows = attended[h * TOK + chunk * ROWS : h * TOK + (chunk + 1) * ROWS]
-            att[chunk % 2, chunk // 2, :, pl.ds(h * HEAD, HEAD)] = rows.astype(BF16)
-
     att_copy = remote(att.at[1 - parity], att_in, a_ss.at[0], a_rs.at[0], twin)
-    att_copy.start()
+    for side in range(2):
+        which = 1 - parity if side == 0 else parity
+        for k in range(NPAIR):
+            for h in range(2):
+                even = attended[h * TOK + 2 * k * ROWS : h * TOK + (2 * k + 1) * ROWS]
+                odd = attended[h * TOK + (2 * k + 1) * ROWS : h * TOK + (2 * k + 2) * ROWS]
+                att[which, k, :, pl.ds(h * HEAD, HEAD)] = jnp.where(which == 0, even, odd).astype(BF16)
+        if side == 0:
+            att_copy.start()
 
     def project_out(rows, depth_start, piece):
         columns = pl.ds(piece * WIDE, WIDE)

time: 104 us -> 104 us (level)
  no operation moved by 1% of the time
where the time goes in v5:
time: 104 us
  Pallas kernels  102 us (98%)
  local copies, waits for them, and re-layouts  1.54 us (1%)
    pallas_call x1, Pallas kernels, body(): pl.pallas_call(kernel, out_shape=jax.ShapeDtypeStruct((TOK, 2 * HEAD), BF...  102 us

profile of v5, /device:TPU:7, one launch (start us, length us, event | category | flops | bytes accessed | tf_op | source)
XLA Modules:
  0.0 103.9 jit_solution(9092459288729158420)
XLA Ops:
  0.0 102.3 %shard_map.82 = bf16[192,256]{1,0:T(8,128)(2,1)} custom-call(bf16[192,4096]{1,0:T(8,128)(2,1)} %hidden.1, bf16[192,256]{1,0:T(8,128)(2,1)} %query.1, bf16[192,128]{1,0:T(8,128)(2,1)} %key.1, bf16[192,128]{1,0:T(8,128)(2,1)} %value.1, bf16[256,4096]{1,0:T(8,128)(2,1)} %w_out.1, bf16[4096,256]{1,0:T(8,128)(2,1)} %w_q.1, bf16[4096,256]{1,0:T(8,128)(2,1)} %w_k.1, ...), custom_call_target="tpu_custom_call" | custom-call | tf_op jit(solution)/shard_map/pallas_call | solution.py:531
  102.3 1.5 %copy.10 = bf16[192,256]{1,0:T(8,128)(2,1)} copy(bf16[192,256]{1,0:T(8,128)(2,1)} %shard_map.82) | data formatting | bytes 196608
